TPU v7x, 128 devices: a whole 4x4x4 slice. The times are simulated.
128 devices in a mesh: dom: 32 (over y, x, core), mode: 4 (over z).
Axes of the slice: x: 4, y: 4, z: 4, core: 2. Of those that a mesh axis runs over, the one named last changes fastest.
Arguments:
- mode_shapes: bfloat16 [128, 6, 32768], P('mode', None, 'dom'), may hold values from -0.29882812 to 0.29882812
- eigenvalues: float32 [128], replicated, may hold values from 0.7 to 192, as said below
- mode_weights: float32 [128], P('mode'), may hold values from 0.1 to 1
- stiff_deriv: bfloat16 [24, 24, 49152], P(None, None, 'dom'), as said below
- mass_ref: bfloat16 [24, 24], replicated, as said below
- mass_scale: float32 [49152], P('dom'), may hold values from 0.5 to 2
- connectivity: int32 [4, 49152], P(None, 'dom'), may hold values from 0 to 1087, as said below
- design_owner: int32 [49152], P('dom'), may hold values from 0 to 20479, as said below
- direction: float32 [20480], P('dom'), may hold values from -0.12 to 0.12
Outputs:
- hess_vec: float32 [20480], P('dom')
- eig_deriv: float32 [128], P('mode')
Inputs may be any that keep to these rules, and one draw needn't show every extreme that they name: Distinct eigenvalues, increasing with the mode index, neighbours at least 0.4 apart. `stiff_deriv`: symmetric 24 by 24 matrices with a positive diagonal. `mass_ref`: Symmetric, with a positive diagonal. `connectivity`: index into the extended node list of the element's device: the 32 upper rim nodes of the lower neighbour, the device's own 1024 nodes, then the 32 lower rim nodes of the upper neighbour. The corners of one element lie within 64 positions of one another. Elements of the first device never name the lower rim; those of the last never name the upper rim. `design_owner`: an element of index r of dom has its design variable in the blocks of 640 design variables of indices r - 1, r or r + 1 of dom.
All inputs are finite; a program needn't handle non-finite values.
Results may differ from a plain program's by a relative error of at most 0.01.
Values may be sent and summed in bfloat16 or wider, within the bound.
No kernel may reach another device: no remote copies, remote signals or barrier semaphores. Data moves between devices by JAX's collectives and lax.ppermute only.
A program may use at most 64 MiB of HBM per device.

v0:
```python
import jax
import jax.numpy as jnp
from jax import lax
from jax.sharding import PartitionSpec as P

EBLK = 256
H = 32


def with_halo(block, sides, width):
    for axis, dim in sides:
        count = lax.axis_size(axis)
        forward = [(i, i + 1) for i in range(count - 1)]
        backward = [(target, source) for source, target in forward]
        low = lax.ppermute(
            lax.slice_in_dim(block, block.shape[dim] - width, None, axis=dim), axis, forward
        )
        high = lax.ppermute(lax.slice_in_dim(block, 0, width, axis=dim), axis, backward)
        block = jnp.concatenate([low, block, high], axis=dim)
    return block


def shifted(value, axis, steps):
    count = lax.axis_size(axis)
    leading, last = (max(0, -steps), min(count, count - steps))
    return lax.ppermute(value, axis, [(source, source + steps) for source in range(leading, last)])


def element_dofs(field, element_nodes):
    picked = field[:, :, element_nodes]
    return picked.reshape(field.shape[0], 24, element_nodes.shape[1])


def on_device(
    mode_shapes,
    eigenvalues,
    mode_weights,
    stiff_deriv,
    mass_ref,
    mass_scale,
    connectivity,
    design_owner,
    direction,
):
    mode_dev = mode_shapes.shape[0]
    elem_dev = connectivity.shape[1]
    des_dev = direction.shape[0]
    mode_start = lax.axis_index("mode") * mode_dev
    dom_rank = lax.axis_index("dom")
    all_modes = lax.all_gather(mode_shapes, "mode", axis=0, tiled=True)
    extended = with_halo(all_modes, (("dom", 2),), H)
    ext_mine = lax.dynamic_slice_in_dim(extended, mode_start, mode_dev, 0)
    eig_mine = lax.dynamic_slice_in_dim(eigenvalues, mode_start, mode_dev, 0)
    dir_table = with_halo(direction, (("dom", 0),), des_dev)
    local_owner = design_owner - (dom_rank - 1) * des_dev
    table_len = 3 * des_dev
    elem_dir = dir_table[local_owner]
    elem_dirmass = elem_dir * mass_scale
    num_blocks = elem_dev // EBLK

    def gram_block(block, totals):
        start = block * EBLK
        element_nodes = lax.dynamic_slice_in_dim(connectivity, start, EBLK, 1)
        matrices = lax.dynamic_slice_in_dim(stiff_deriv, start, EBLK, 2)
        dir_block = lax.dynamic_slice_in_dim(elem_dir, start, EBLK, 0)
        dirmass_block = lax.dynamic_slice_in_dim(elem_dirmass, start, EBLK, 0)
        all_dofs = element_dofs(extended, element_nodes)
        mine_dofs = lax.dynamic_slice_in_dim(all_dofs, mode_start, mode_dev, 0)
        stiff_part = jnp.einsum(
            "abe,mbe->mae", matrices, mine_dofs, preferred_element_type=jnp.float32
        )
        force_k = (dir_block * stiff_part).astype(jnp.bfloat16)
        mass_shapes = jnp.einsum(
            "ab,mbe->mae", mass_ref, mine_dofs, preferred_element_type=jnp.float32
        )
        force_m = (dirmass_block * mass_shapes).astype(jnp.bfloat16)
        dims = (((1, 2), (1, 2)), ((), ()))
        stiff_gram = lax.dot_general(all_dofs, force_k, dims, preferred_element_type=jnp.float32)
        mass_gram = lax.dot_general(all_dofs, force_m, dims, preferred_element_type=jnp.float32)
        return (totals[0] + stiff_gram, totals[1] + mass_gram)

    empty = jnp.zeros((extended.shape[0], mode_dev), jnp.float32)
    stiff_gram, mass_gram = lax.fori_loop(0, num_blocks, gram_block, (empty, empty))
    stiff_gram, mass_gram = lax.psum((stiff_gram, mass_gram), "dom")
    resid = stiff_gram - eig_mine[None, :] * mass_gram
    mass_diag = jnp.diagonal(lax.dynamic_slice_in_dim(mass_gram, mode_start, mode_dev, 0))
    eig_deriv = jnp.diagonal(lax.dynamic_slice_in_dim(resid, mode_start, mode_dev, 0))
    row_index = jnp.arange(extended.shape[0], dtype=jnp.int32)[:, None]
    col_index = mode_start + jnp.arange(mode_dev, dtype=jnp.int32)[None, :]
    diagonal_mask = row_index == col_index
    spacing = eig_mine[None, :] - eigenvalues[:, None]
    combiner = jnp.where(
        diagonal_mask, -0.5 * mass_diag[None, :], resid / jnp.where(diagonal_mask, 1.0, spacing)
    ).astype(jnp.bfloat16)
    deriv_ext = jnp.einsum(
        "ji,jcn->icn", combiner, extended, preferred_element_type=jnp.float32
    ).astype(jnp.bfloat16)

    def energy_block(block, energy):
        start = block * EBLK
        element_nodes = lax.dynamic_slice_in_dim(connectivity, start, EBLK, 1)
        matrices = lax.dynamic_slice_in_dim(stiff_deriv, start, EBLK, 2)
        mass_block = lax.dynamic_slice_in_dim(mass_scale, start, EBLK, 0)
        shapes = element_dofs(ext_mine, element_nodes)
        deriv_dofs = element_dofs(deriv_ext, element_nodes)
        stiff_q = jnp.einsum(
            "abe,mbe->mae", matrices, deriv_dofs, preferred_element_type=jnp.float32
        )
        mass_q = jnp.einsum("ab,mbe->mae", mass_ref, deriv_dofs, preferred_element_type=jnp.float32)
        mass_shapes = jnp.einsum(
            "ab,mbe->mae", mass_ref, shapes, preferred_element_type=jnp.float32
        )
        term_k = jnp.sum(shapes * stiff_q, axis=1)
        term_m = jnp.sum(shapes * mass_q, axis=1)
        term_p = jnp.sum(shapes * mass_shapes, axis=1)
        inner = 2.0 * term_k - mass_block[None, :] * (
            2.0 * eig_mine[:, None] * term_m + eig_deriv[:, None] * term_p
        )
        values = jnp.sum(mode_weights[:, None] * inner, axis=0)
        return lax.dynamic_update_slice_in_dim(energy, values, start, 0)

    energy = lax.fori_loop(0, num_blocks, energy_block, jnp.zeros((elem_dev,), jnp.float32))
    local_sums = jax.ops.segment_sum(energy, local_owner, num_segments=table_len)
    from_upper = shifted(local_sums[:des_dev], "dom", -1)
    from_lower = shifted(local_sums[2 * des_dev :], "dom", 1)
    owned = local_sums[des_dev : 2 * des_dev] + from_upper + from_lower
    hess_vec = lax.psum(owned, "mode")
    return (hess_vec, eig_deriv)


def solution(mesh):
    return jax.shard_map(
        on_device,
        mesh=mesh,
        in_specs=(
            P("mode", None, "dom"),
            P(),
            P("mode"),
            P(None, None, "dom"),
            P(),
            P("dom"),
            P(None, "dom"),
            P("dom"),
            P("dom"),
        ),
        out_specs=(P("dom"), P("mode")),
        check_vma=False,
    )
```

profile of v0, /device:TPU:2, one launch (start us, length us, event | category | flops | bytes accessed | tf_op | source)
XLA Modules:
  0.0 601.9 jit_solution(8886556330250387583)
XLA Ops:
  9.8 3.6 collective-permute-start.3
  13.5 10.5 %copy.100 = bf16[24,24,1536]{1,0,2:T(8,128)(2,1)} copy(bf16[24,24,1536]{2,1,0:T(8,128)(2,1)} %param.16) | data formatting | bytes 3538944
  25.8 13.0 %all-gather.2.cloned.1.call-done = bf16[128,6,1024]{2,0,1:T(8,128)(2,1)} async-done(((bf16[32,6,1024]{2,0,1:T(8,128)(2,1)}), bf16[128,6,1024]{2,0,1:T(8,128)(2,1)}) %all-gather.2.cloned.1.call-update) | async-done | bytes 1572880 | tf_op jit(solution)/shard_map/all_gather | solution.py:50
  42.7 3.6 collective-permute-start.1
  46.4 11.8 %gather_fusion.3 = f32[1536]{0:T(1024)} fusion(f32[1920]{0:T(1024)S(1)} %pad_maximum_fusion.1, s32[2048]{0:T(1024)S(1)} %pad_clamp_fusion), kind=kCustom, calls=%fused_computation.3 | custom fusion | bytes 18432 | tf_op jit(solution)/shard_map/gather | solution.py:57
  60.6 7.4 %copy.99 = bf16[128,6,1088]{0,1,2:T(8,128)(2,1)} copy(bf16[128,6,1088]{0,2,1:T(8,128)(2,1)S(1)} %pad_maximum_fusion) | data formatting | bytes 3342336
  68.0 7.3 %copy.101 = bf16[32,6,1088]{0,1,2:T(8,128)(2,1)} copy(bf16[32,6,1088]{0,2,1:T(8,128)(2,1)S(1)} %constant_dynamic-slice_fusion.3) | data formatting | bytes 835584 | tf_op jit(solution)/shard_map/while | solution.py:122
  75.3 145.4 %while.32 = (s32[]{:T(128)}, f32[128,32]{0,1:T(8,128)}, f32[128,32]{0,1:T(8,128)}, s32[4,1536]{1,0:T(4,128)}, bf16[128,6,1088]{0,1,2:T(8,128)(2,1)}, /*index=5*/...) while((s32[]{:T(128)}, f32[128,32]{0,1:T(8,128)}, ...), condition=%wide.region_1.0_spmd.clone, body=%wide.region_0.0_spmd.clone.sunk | while | flops 120344584 | bytes 15175058 | solution.py:83
  77.5 9.3 %gather_fusion.2 = bf16[1024,128,6]{1,2,0:T(8,128)(2,1)} fusion(bf16[128,6,1088]{0,1,2:T(8,128)(2,1)} %get-tuple-element.781, s32[1024]{0:T(1024)S(1)} %broadcast_clamp_fusion.5), kind=kCustom, calls=%fused_computation.clone.clone.1 | custom fusion | bytes 3149824 | tf_op jit(solution)/shard_map/while/body/eval_jaxpr/gather | solution.py:30
  86.8 3.6 copy.141
  101.8 9.3 %gather_fusion.2 = bf16[1024,128,6]{1,2,0:T(8,128)(2,1)} fusion(bf16[128,6,1088]{0,1,2:T(8,128)(2,1)} %get-tuple-element.781, s32[1024]{0:T(1024)S(1)} %broadcast_clamp_fusion.5), kind=kCustom, calls=%fused_computation.clone.clone.1 | custom fusion | bytes 3149824 | tf_op jit(solution)/shard_map/while/body/eval_jaxpr/gather | solution.py:30
  111.0 3.6 copy.141
  126.0 9.3 %gather_fusion.2 = bf16[1024,128,6]{1,2,0:T(8,128)(2,1)} fusion(bf16[128,6,1088]{0,1,2:T(8,128)(2,1)} %get-tuple-element.781, s32[1024]{0:T(1024)S(1)} %broadcast_clamp_fusion.5), kind=kCustom, calls=%fused_computation.clone.clone.1 | custom fusion | bytes 3149824 | tf_op jit(solution)/shard_map/while/body/eval_jaxpr/gather | solution.py:30
  135.2 3.6 copy.141
  150.2 9.3 %gather_fusion.2 = bf16[1024,128,6]{1,2,0:T(8,128)(2,1)} fusion(bf16[128,6,1088]{0,1,2:T(8,128)(2,1)} %get-tuple-element.781, s32[1024]{0:T(1024)S(1)} %broadcast_clamp_fusion.5), kind=kCustom, calls=%fused_computation.clone.clone.1 | custom fusion | bytes 3149824 | tf_op jit(solution)/shard_map/while/body/eval_jaxpr/gather | solution.py:30
  159.5 3.6 copy.141
  174.5 9.3 %gather_fusion.2 = bf16[1024,128,6]{1,2,0:T(8,128)(2,1)} fusion(bf16[128,6,1088]{0,1,2:T(8,128)(2,1)} %get-tuple-element.781, s32[1024]{0:T(1024)S(1)} %broadcast_clamp_fusion.5), kind=kCustom, calls=%fused_computation.clone.clone.1 | custom fusion | bytes 3149824 | tf_op jit(solution)/shard_map/while/body/eval_jaxpr/gather | solution.py:30
  183.7 3.6 copy.141
  198.7 9.3 %gather_fusion.2 = bf16[1024,128,6]{1,2,0:T(8,128)(2,1)} fusion(bf16[128,6,1088]{0,1,2:T(8,128)(2,1)} %get-tuple-element.781, s32[1024]{0:T(1024)S(1)} %broadcast_clamp_fusion.5), kind=kCustom, calls=%fused_computation.clone.clone.1 | custom fusion | bytes 3149824 | tf_op jit(solution)/shard_map/while/body/eval_jaxpr/gather | solution.py:30
  207.9 3.6 copy.141
  220.7 122.2 %all-reduce = (f32[128,32]{0,1:T(8,128)S(1)}, f32[128,32]{0,1:T(8,128)S(1)}) all-reduce(f32[128,32]{0,1:T(8,128)} %get-tuple-element.423, f32[128,32]{0,1:T(8,128)} %get-tuple-element.422), channel_id=1, replica_groups=mesh['dom'=32,'mode'=4] {'dom'}, use_global_device_ids=true, to_apply=%region_3.0 | all-reduce | flops 8192 | bytes 65536 | tf_op jit(solution)/shard_map/psum | solution.py:84
  350.0 215.5 %while.31 = (s32[]{:T(128)}, f32[1536]{0:T(1024)S(1)}, f32[32]{0:T(128)S(1)}, s32[4,1536]{1,0:T(4,128)}, bf16[32,6,1088]{0,1,2:T(8,128)(2,1)}, /*index=5*/bf16[3...) while((s32[]{:T(128)}, f32[1536]{0:T(1024)S(1)}, ...), condition=%wide.region_9.10_spmd, body=%wide.region_4.9_spmd.sunk | while | flops 29929252 | bytes 18916456 | solution.py:122
  351.5 5.0 gather_fusion.1
  360.1 9.3 %gather_fusion = bf16[1024,32,6]{1,2,0:T(8,128)(2,1)} fusion(bf16[32,6,1088]{0,1,2:T(8,128)(2,1)} %get-tuple-element.825, s32[1024]{0:T(1024)S(1)} %broadcast_clamp_fusion.4), kind=kCustom, calls=%fused_computation.1.clone.1 | custom fusion | bytes 790528 | tf_op jit(solution)/shard_map/while/body/eval_jaxpr/gather | solution.py:30
  369.3 3.6 copy.130
  381.1 4.3 fusion.85
  387.4 5.0 gather_fusion.1
  396.0 9.3 %gather_fusion = bf16[1024,32,6]{1,2,0:T(8,128)(2,1)} fusion(bf16[32,6,1088]{0,1,2:T(8,128)(2,1)} %get-tuple-element.825, s32[1024]{0:T(1024)S(1)} %broadcast_clamp_fusion.4), kind=kCustom, calls=%fused_computation.1.clone.1 | custom fusion | bytes 790528 | tf_op jit(solution)/shard_map/while/body/eval_jaxpr/gather | solution.py:30
  405.3 3.6 copy.130
  417.1 4.3 fusion.85
  423.3 5.0 gather_fusion.1
  431.9 9.3 %gather_fusion = bf16[1024,32,6]{1,2,0:T(8,128)(2,1)} fusion(bf16[32,6,1088]{0,1,2:T(8,128)(2,1)} %get-tuple-element.825, s32[1024]{0:T(1024)S(1)} %broadcast_clamp_fusion.4), kind=kCustom, calls=%fused_computation.1.clone.1 | custom fusion | bytes 790528 | tf_op jit(solution)/shard_map/while/body/eval_jaxpr/gather | solution.py:30
  441.2 3.6 copy.130
  453.0 4.3 fusion.85
  459.3 5.0 gather_fusion.1
  467.9 9.3 %gather_fusion = bf16[1024,32,6]{1,2,0:T(8,128)(2,1)} fusion(bf16[32,6,1088]{0,1,2:T(8,128)(2,1)} %get-tuple-element.825, s32[1024]{0:T(1024)S(1)} %broadcast_clamp_fusion.4), kind=kCustom, calls=%fused_computation.1.clone.1 | custom fusion | bytes 790528 | tf_op jit(solution)/shard_map/while/body/eval_jaxpr/gather | solution.py:30
  477.1 3.6 copy.130
  488.9 4.3 fusion.85
  495.2 5.0 gather_fusion.1
  503.8 9.3 %gather_fusion = bf16[1024,32,6]{1,2,0:T(8,128)(2,1)} fusion(bf16[32,6,1088]{0,1,2:T(8,128)(2,1)} %get-tuple-element.825, s32[1024]{0:T(1024)S(1)} %broadcast_clamp_fusion.4), kind=kCustom, calls=%fused_computation.1.clone.1 | custom fusion | bytes 790528 | tf_op jit(solution)/shard_map/while/body/eval_jaxpr/gather | solution.py:30
  513.1 3.6 copy.130
  524.9 4.3 fusion.85
  531.1 5.0 gather_fusion.1
  539.7 9.3 %gather_fusion = bf16[1024,32,6]{1,2,0:T(8,128)(2,1)} fusion(bf16[32,6,1088]{0,1,2:T(8,128)(2,1)} %get-tuple-element.825, s32[1024]{0:T(1024)S(1)} %broadcast_clamp_fusion.4), kind=kCustom, calls=%fused_computation.1.clone.1 | custom fusion | bytes 790528 | tf_op jit(solution)/shard_map/while/body/eval_jaxpr/gather | solution.py:30
  560.7 4.3 fusion.85
  565.5 8.8 %scatter_custom_fusion = f32[1920]{0:T(1024)S(1)} fusion(s32[1536]{0:T(1024)} %get-tuple-element.610, f32[1536]{0:T(1024)S(1)} %get-tuple-element.424, f32[]{:T(128)} %constant.130.clone.1), kind=kCustom, calls=%fused_computation.58 | custom fusion | flops 1536 | bytes 8192 | tf_op jit(solution)/shard_map/scatter-add | solution.py:123
  578.7 6.5 %collective-permute-done.5 = f32[640]{0:T(1024)S(1)} collective-permute-done((f32[640]{0:T(1024)S(1)}, f32[640]{0:T(1024)S(1)}, u32[]{:S(2)}, u32[]{:S(2)}) %collective-permute-start.5) | collective-permute-done | bytes 2592 | tf_op jit(solution)/shard_map/ppermute | solution.py:26
  585.2 9.9 %psum.23 = f32[640]{0:T(1024)} all-reduce(f32[640]{0:T(1024)S(1)} %fusion.40), channel_id=1, replica_groups=mesh['dom'=32,'mode'=4] {'mode'}, use_global_device_ids=true, to_apply=%region_11.12 | all-reduce | flops 640 | bytes 5120 | tf_op jit(solution)/shard_map/psum | solution.py:127
  (273 shorter events, 176.2 us)
Async XLA Ops:
  7.2 31.6 %all-gather.2.cloned.1.call-start = ((), (), s32[]{:S(2)}) async-start(), calls=%async_computation | async-start | bytes 1966080 | tf_op jit(solution)/shard_map/all_gather | solution.py:50
  7.9 38.4 %collective-permute-start.2 = (f32[640]{0:T(1024)}, f32[640]{0:T(1024)S(1)}, u32[]{:S(2)}, u32[]{:S(2)}) collective-permute-start(f32[640]{0:T(1024)} %param.21), channel_id=1, source_target_pairs={{0,4},{4,8},{8,12},{12,16},{16,20},{20,24},{24,28},{28,32},{32,36}... | collective-permute-start | bytes 7688 | tf_op jit(solution)/shard_map/ppermute | solution.py:15
  9.8 36.5 %collective-permute-start.3 = (f32[640]{0:T(1024)}, f32[640]{0:T(1024)S(1)}, u32[]{:S(2)}, u32[]{:S(2)}) collective-permute-start(f32[640]{0:T(1024)} %param.21), channel_id=1, source_target_pairs={{4,0},{8,4},{12,8},{16,12},{20,16},{24,20},{28,24},{32,28},{36,32}... | collective-permute-start | bytes 7688 | tf_op jit(solution)/shard_map/ppermute | solution.py:18
  13.5 10.5 %copy-start.13 = (f32[128]{0:T(128)S(1)}, f32[128]{0:T(128)}, u32[]{:S(2)}) copy-start(f32[128]{0:T(128)} %param.14) | copy-start | bytes 1540
  13.5 11.7 %copy-start.10 = (s32[1536]{0:T(1024)S(1)}, s32[1536]{0:T(1024)}, u32[]{:S(2)}) copy-start(s32[1536]{0:T(1024)} %param.20) | copy-start | bytes 18436
  25.8 20.5 %copy-start.11 = (f32[640]{0:T(1024)S(1)}, f32[640]{0:T(1024)}, u32[]{:S(2)}) copy-start(f32[640]{0:T(1024)} %param.21) | copy-start | bytes 7684
  40.7 18.7 %copy-start.1 = (bf16[128,6,1024]{0,2,1:T(8,128)(2,1)}, bf16[128,6,1024]{0,2,1:T(8,128)(2,1)S(1)}, u32[]{:S(2)}) copy-start(bf16[128,6,1024]{0,2,1:T(8,128)(2,1)S(1)} %copy.96) | copy-start | bytes 4718596
  40.7 18.7 %collective-permute-start = (bf16[128,6,32]{0,2,1:T(8,128)(2,1)S(1)}, bf16[128,6,32]{0,2,1:T(8,128)(2,1)S(1)}, u32[]{:S(2)}, u32[]{:S(2)}) collective-permute-start(bf16[128,6,32]{0,2,1:T(8,128)(2,1)S(1)} %get-tuple-element.611), channel_id=1, source_target_pairs={{0,4},{4,8},{8,12},{12,16},{16,20},{20,24},{24,28},{28,32},{32,36}... | collective-permute-start | bytes 147464 | tf_op jit(solution)/shard_map/ppermute | solution.py:15
  42.7 16.8 %collective-permute-start.1 = (bf16[128,6,32]{0,2,1:T(8,128)(2,1)S(1)}, bf16[128,6,32]{0,2,1:T(8,128)(2,1)S(1)}, u32[]{:S(2)}, u32[]{:S(2)}) collective-permute-start(bf16[128,6,32]{0,2,1:T(8,128)(2,1)S(1)} %get-tuple-element.612), channel_id=1, source_target_pairs={{4,0},{8,4},{12,8},{16,12},{20,16},{24,20},{28,24},{32,28},{36,32}... | collective-permute-start | bytes 147464 | tf_op jit(solution)/shard_map/ppermute | solution.py:18
  46.4 11.8 %copy-start.7 = (f32[1536]{0:T(1024)S(1)}, f32[1536]{0:T(1024)}, u32[]{:S(2)}) copy-start(f32[1536]{0:T(1024)} %param.18) | copy-start | bytes 18436
  59.4 0.6 copy-start.5
  59.5 0.6 copy-start.6
  68.0 7.3 %copy-start.2 = (bf16[24,24]{1,0:T(8,128)(2,1)S(1)}, bf16[24,24]{1,0:T(8,128)(2,1)}, u32[]{:S(2)}) copy-start(bf16[24,24]{1,0:T(8,128)(2,1)} %param.17) | copy-start | bytes 3460
  96.2 2.1 copy-start.3
  98.9 0.6 copy-start.4
  120.4 2.1 copy-start.3
  123.2 0.6 copy-start.4
  144.6 2.1 copy-start.3
  147.4 0.6 copy-start.4
  168.9 2.1 copy-start.3
  171.6 0.6 copy-start.4
  193.1 2.1 copy-start.3
  195.9 0.6 copy-start.4
  217.3 2.1 copy-start.3
  220.1 0.6 copy-start.4
  347.3 2.6 copy-start.9
  347.4 2.6 copy-start.12
  376.7 2.2 copy-start
  412.7 2.2 copy-start
  448.6 2.2 copy-start
  484.5 2.2 copy-start
  520.5 2.2 copy-start
  556.4 2.2 copy-start
  565.5 29.6 %copy-start.8 = (f32[32]{0:T(128)}, f32[32]{0:T(128)S(1)}, u32[]{:S(2)}) copy-start(f32[32]{0:T(128)S(1)} %get-tuple-element.846) | copy-start | bytes 388
  574.3 4.3 collective-permute-start.4
  576.3 8.9 %collective-permute-start.5 = (f32[640]{0:T(1024)S(1)}, f32[640]{0:T(1024)S(1)}, u32[]{:S(2)}, u32[]{:S(2)}) collective-permute-start(f32[640]{0:T(1024)S(1)} %get-tuple-element.614), channel_id=1, source_target_pairs={{0,4},{4,8},{8,12},{12,16},{16,20},{20,24},{24,28},{28,32},{32,36}... | collective-permute-start | bytes 7688 | tf_op jit(solution)/shard_map/ppermute | solution.py:26
Sparse Core Ops, SparseCore 0:
  9.7 29.0 all-gather.1
where the time goes:
time: 605 us; the launch traced here: 602 us
  local copies, waits for them, and re-layouts  318 us (53%)
  blocking collectives  132 us (22%)
  matrix products  54.7 us (9%)
  other arithmetic  46.7 us (8%)
  waiting for transfers between devices  20.1 us (3%)
  starting transfers between devices  15.5 us (3%)
  between operations  14.3 us (2%)
    gather x42, local copies, waits for them, and re-layouts, element_dofs(): picked = field[:, :, element_nodes]  193 us
    psum x1, blocking collectives, on_device(): stiff_gram, mass_gram = lax.psum((stiff_gram, mass_gram), 'dom')  122 us
    reduce_sum x6, other arithmetic, energy_block(): term_m = jnp.sum(shapes * mass_q, axis=1)  25.5 us
    dot_general x6, matrix products, gram_block(): lax.dot_general(all_dofs, force_k, dims, preferred_element_type=jnp.float32)  19.3 us
    unnamed x24, local copies, waits for them, and re-layouts  18.4 us
    dot_general x6, matrix products, energy_block(): jnp.einsum('abe,mbe->mae', matrices, deriv_dofs, preferred_element_type=j...  14.3 us
    dot_general x6, local copies, waits for them, and re-layouts, energy_block(): jnp.einsum('ab,mbe->mae', mass_ref, shapes, preferred_element_type=jnp.fl...  13.3 us
    dot_general x6, local copies, waits for them, and re-layouts, energy_block(): jnp.einsum('ab,mbe->mae', mass_ref, deriv_dofs, preferred_element_type=jn...  13 us
  transfers between devices with their start and end apart: 7, of which 2 were waited for; matrix products, arithmetic and copies ran while one was open for 5% of the time, Pallas kernels for 0%

commit v1 on v0

--- a/solution.py
+++ b/solution.py
@@ -47,7 +47,12 @@
     des_dev = direction.shape[0]
     mode_start = lax.axis_index("mode") * mode_dev
     dom_rank = lax.axis_index("dom")
-    all_modes = lax.all_gather(mode_shapes, "mode", axis=0, tiled=True)
+    ring = [mode_shapes]
+    for hop in range(3):
+        ring.append(lax.ppermute(ring[-1], "mode", [(dev, (dev + 1) % 4) for dev in range(4)]))
+    all_modes = jnp.roll(
+        jnp.concatenate(ring[::-1], axis=0), (lax.axis_index("mode") + 1) * ring[0].shape[0], axis=0
+    )
     extended = with_halo(all_modes, (("dom", 2),), H)
     ext_mine = lax.dynamic_slice_in_dim(extended, mode_start, mode_dev, 0)
     eig_mine = lax.dynamic_slice_in_dim(eigenvalues, mode_start, mode_dev, 0)

time: 605 us -> 619 us (1.023)
  local copies, waits for them, and re-layouts: 318 us -> 339 us
  between operations: 14.3 us -> 0.9 us
    ppermute x0 -> x3, waiting for transfers between devices: none -> 16.2 us  [on_device(): lax.ppermute(ring[-1], 'mode', [(dev, (dev + 1) % 4) for dev in range(4)])]
    all_gather x1 -> x0, waiting for transfers between devices: 13 us -> none  [on_device(): all_modes = lax.all_gather(mode_shapes, 'mode', axis=0, tiled=True)]
    concatenate x0 -> x1, local copies, waits for them, and re-layouts: none -> 12.3 us  [on_device(): jnp.roll(jnp.concatenate(ring[::-1], axis=0), (lax.axis_index('mode') + 1...]
    ppermute x0 -> x3, local copies, waits for them, and re-layouts: none -> 6.47 us  [on_device(): lax.ppermute(ring[-1], 'mode', [(dev, (dev + 1) % 4) for dev in range(4)])]
    unnamed x24 -> x27, local copies, waits for them, and re-layouts: 18.4 us -> 19.1 us
  transfers between devices with their start and end apart: 7 -> 9, of which waited for: 2 -> 3; matrix products, arithmetic and copies ran while one was open for 5% -> 5% of each run, Pallas kernels for 0% -> 0%
where the time goes in v1:
time: 619 us; the launch traced here: 616 us
  local copies, waits for them, and re-layouts  339 us (55%)
  blocking collectives  133 us (21%)
  matrix products  54.7 us (9%)
  other arithmetic  47.2 us (8%)
  waiting for transfers between devices  22.7 us (4%)
  starting transfers between devices  17.4 us (3%)
    gather x42, local copies, waits for them, and re-layouts, element_dofs(): picked = field[:, :, element_nodes]  193 us
    psum x1, blocking collectives, on_device(): stiff_gram, mass_gram = lax.psum((stiff_gram, mass_gram), 'dom')  122 us
    reduce_sum x6, other arithmetic, energy_block(): term_m = jnp.sum(shapes * mass_q, axis=1)  25.5 us
    dot_general x6, matrix products, gram_block(): lax.dot_general(all_dofs, force_k, dims, preferred_element_type=jnp.float32)  19.3 us
    unnamed x27, local copies, waits for them, and re-layouts  19.1 us
    ppermute x3, waiting for transfers between devices, on_device(): lax.ppermute(ring[-1], 'mode', [(dev, (dev + 1) % 4) for dev in range(4)])  16.2 us
    dot_general x6, matrix products, energy_block(): jnp.einsum('abe,mbe->mae', matrices, deriv_dofs, preferred_element_type=j...  14.3 us
    dot_general x6, local copies, waits for them, and re-layouts, energy_block(): jnp.einsum('ab,mbe->mae', mass_ref, shapes, preferred_element_type=jnp.fl...  13.2 us
  transfers between devices with their start and end apart: 9, of which 3 were waited for; matrix products, arithmetic and copies ran while one was open for 5% of the time, Pallas kernels for 0%

profile of v1, /device:TPU:2, one launch (start us, length us, event | category | flops | bytes accessed | tf_op | source)
XLA Modules:
  0.0 615.7 jit_solution(10777555970320524752)
XLA Ops:
  2.6 11.4 %collective-permute-done = bf16[32,6,1024]{2,0,1:T(8,128)(2,1)S(1)} collective-permute-done((bf16[32,6,1024]{2,0,1:T(8,128)(2,1)}, bf16[32,6,1024]{2,0,1:T(8,128)(2,1)S(1)}, u32[]{:S(2)}, u32[]{:S(2)}) %collective-permute-start) | collective-permute-done | bytes 393248 | tf_op jit(solution)/shard_map/ppermute | solution.py:52
  16.0 3.6 collective-permute-start.6
  21.0 4.7 collective-permute-done.1
  28.0 8.9 %copy.116 = bf16[24,24,1536]{1,0,2:T(8,128)(2,1)} copy(bf16[24,24,1536]{2,1,0:T(8,128)(2,1)S(1)} %copy-done.2) | data formatting | bytes 3538944
  37.6 11.7 %gather_fusion.3 = f32[1536]{0:T(1024)} fusion(f32[1920]{0:T(1024)S(1)} %pad_maximum_fusion.1, s32[2048]{0:T(1024)S(1)} %pad_clamp_fusion), kind=kCustom, calls=%fused_computation.3 | custom fusion | bytes 18432 | tf_op jit(solution)/shard_map/gather | solution.py:62
  57.1 12.3 %concatenate.17 = bf16[256,6,1024]{0,2,1:T(8,128)(2,1)} concatenate(bf16[32,6,1024]{0,2,1:T(8,128)(2,1)} %copy.107, bf16[32,6,1024]{0,2,1:T(8,128)(2,1)} %copy.108, bf16[32,6,1024]{0,2,1:T(8,128)(2,1)S(1)} %copy.109, bf16[32,6,1024]{0,2,1:T(8,128)(2,1)S(1)} %copy.110, bf16[32,6,1024]{0,2,1:T(8,128)(2,1)} %copy.107, bf16[32,6,1024]{0,2,1:T(8,128)(2,1)} %copy.108, ...), dimensions={0} | concatenate | bytes 6291456 | tf_op jit(solution)/shard_map/jit(_roll_dynamic)/concatenate | solution.py:53
  72.4 3.6 collective-permute-start.4
  80.2 7.3 %copy.115 = bf16[128,6,1088]{0,1,2:T(8,128)(2,1)} copy(bf16[128,6,1088]{0,2,1:T(8,128)(2,1)S(1)} %pad_maximum_fusion) | data formatting | bytes 3342336
  87.6 7.3 %copy.117 = bf16[32,6,1088]{0,1,2:T(8,128)(2,1)} copy(bf16[32,6,1088]{0,2,1:T(8,128)(2,1)S(1)} %constant_dynamic-slice_fusion.5) | data formatting | bytes 835584 | tf_op jit(solution)/shard_map/while | solution.py:127
  94.9 145.5 %while.32 = (s32[]{:T(128)}, f32[128,32]{0,1:T(8,128)}, f32[128,32]{0,1:T(8,128)}, s32[4,1536]{1,0:T(4,128)}, bf16[128,6,1088]{0,1,2:T(8,128)(2,1)}, /*index=5*/...) while((s32[]{:T(128)}, f32[128,32]{0,1:T(8,128)}, ...), condition=%wide.region_1.2_spmd.clone, body=%wide.region_0.1_spmd.clone.sunk | while | flops 120344584 | bytes 15175058 | solution.py:88
  97.1 9.3 %gather_fusion.2 = bf16[1024,128,6]{1,2,0:T(8,128)(2,1)} fusion(bf16[128,6,1088]{0,1,2:T(8,128)(2,1)} %get-tuple-element.781, s32[1024]{0:T(1024)S(1)} %broadcast_clamp_fusion.5), kind=kCustom, calls=%fused_computation.clone.clone.1 | custom fusion | bytes 3149824 | tf_op jit(solution)/shard_map/while/body/eval_jaxpr/gather | solution.py:30
  106.4 3.6 copy.157
  121.4 9.3 %gather_fusion.2 = bf16[1024,128,6]{1,2,0:T(8,128)(2,1)} fusion(bf16[128,6,1088]{0,1,2:T(8,128)(2,1)} %get-tuple-element.781, s32[1024]{0:T(1024)S(1)} %broadcast_clamp_fusion.5), kind=kCustom, calls=%fused_computation.clone.clone.1 | custom fusion | bytes 3149824 | tf_op jit(solution)/shard_map/while/body/eval_jaxpr/gather | solution.py:30
  130.6 3.6 copy.157
  145.6 9.3 %gather_fusion.2 = bf16[1024,128,6]{1,2,0:T(8,128)(2,1)} fusion(bf16[128,6,1088]{0,1,2:T(8,128)(2,1)} %get-tuple-element.781, s32[1024]{0:T(1024)S(1)} %broadcast_clamp_fusion.5), kind=kCustom, calls=%fused_computation.clone.clone.1 | custom fusion | bytes 3149824 | tf_op jit(solution)/shard_map/while/body/eval_jaxpr/gather | solution.py:30
  154.9 3.6 copy.157
  169.9 9.3 %gather_fusion.2 = bf16[1024,128,6]{1,2,0:T(8,128)(2,1)} fusion(bf16[128,6,1088]{0,1,2:T(8,128)(2,1)} %get-tuple-element.781, s32[1024]{0:T(1024)S(1)} %broadcast_clamp_fusion.5), kind=kCustom, calls=%fused_computation.clone.clone.1 | custom fusion | bytes 3149824 | tf_op jit(solution)/shard_map/while/body/eval_jaxpr/gather | solution.py:30
  179.1 3.6 copy.157
  194.1 9.3 %gather_fusion.2 = bf16[1024,128,6]{1,2,0:T(8,128)(2,1)} fusion(bf16[128,6,1088]{0,1,2:T(8,128)(2,1)} %get-tuple-element.781, s32[1024]{0:T(1024)S(1)} %broadcast_clamp_fusion.5), kind=kCustom, calls=%fused_computation.clone.clone.1 | custom fusion | bytes 3149824 | tf_op jit(solution)/shard_map/while/body/eval_jaxpr/gather | solution.py:30
  203.4 3.6 copy.157
  218.3 9.3 %gather_fusion.2 = bf16[1024,128,6]{1,2,0:T(8,128)(2,1)} fusion(bf16[128,6,1088]{0,1,2:T(8,128)(2,1)} %get-tuple-element.781, s32[1024]{0:T(1024)S(1)} %broadcast_clamp_fusion.5), kind=kCustom, calls=%fused_computation.clone.clone.1 | custom fusion | bytes 3149824 | tf_op jit(solution)/shard_map/while/body/eval_jaxpr/gather | solution.py:30
  227.6 3.6 copy.157
  240.4 122.3 %all-reduce = (f32[128,32]{0,1:T(8,128)S(1)}, f32[128,32]{0,1:T(8,128)S(1)}) all-reduce(f32[128,32]{0,1:T(8,128)} %get-tuple-element.423, f32[128,32]{0,1:T(8,128)} %get-tuple-element.422), channel_id=1, replica_groups=mesh['dom'=32,'mode'=4] {'dom'}, use_global_device_ids=true, to_apply=%region_3.4 | all-reduce | flops 8192 | bytes 65536 | tf_op jit(solution)/shard_map/psum | solution.py:89
  369.8 215.4 %while.31 = (s32[]{:T(128)}, f32[1536]{0:T(1024)S(1)}, f32[32]{0:T(128)S(1)}, s32[4,1536]{1,0:T(4,128)}, bf16[32,6,1088]{0,1,2:T(8,128)(2,1)}, /*index=5*/bf16[3...) while((s32[]{:T(128)}, f32[1536]{0:T(1024)S(1)}, ...), condition=%wide.region_9.10_spmd, body=%wide.region_4.9_spmd.sunk | while | flops 29929252 | bytes 18916456 | solution.py:127
  371.2 5.0 gather_fusion.1
  379.9 9.2 %gather_fusion = bf16[1024,32,6]{1,2,0:T(8,128)(2,1)} fusion(bf16[32,6,1088]{0,1,2:T(8,128)(2,1)} %get-tuple-element.825, s32[1024]{0:T(1024)S(1)} %broadcast_clamp_fusion.4), kind=kCustom, calls=%fused_computation.1.clone.1 | custom fusion | bytes 790528 | tf_op jit(solution)/shard_map/while/body/eval_jaxpr/gather | solution.py:30
  400.9 4.3 fusion.84
  407.2 5.0 gather_fusion.1
  415.8 9.2 %gather_fusion = bf16[1024,32,6]{1,2,0:T(8,128)(2,1)} fusion(bf16[32,6,1088]{0,1,2:T(8,128)(2,1)} %get-tuple-element.825, s32[1024]{0:T(1024)S(1)} %broadcast_clamp_fusion.4), kind=kCustom, calls=%fused_computation.1.clone.1 | custom fusion | bytes 790528 | tf_op jit(solution)/shard_map/while/body/eval_jaxpr/gather | solution.py:30
  425.0 3.6 copy.146
  436.8 4.3 fusion.84
  443.1 5.0 gather_fusion.1
  451.7 9.2 %gather_fusion = bf16[1024,32,6]{1,2,0:T(8,128)(2,1)} fusion(bf16[32,6,1088]{0,1,2:T(8,128)(2,1)} %get-tuple-element.825, s32[1024]{0:T(1024)S(1)} %broadcast_clamp_fusion.4), kind=kCustom, calls=%fused_computation.1.clone.1 | custom fusion | bytes 790528 | tf_op jit(solution)/shard_map/while/body/eval_jaxpr/gather | solution.py:30
  472.7 4.3 fusion.84
  479.0 5.0 gather_fusion.1
  487.6 9.2 %gather_fusion = bf16[1024,32,6]{1,2,0:T(8,128)(2,1)} fusion(bf16[32,6,1088]{0,1,2:T(8,128)(2,1)} %get-tuple-element.825, s32[1024]{0:T(1024)S(1)} %broadcast_clamp_fusion.4), kind=kCustom, calls=%fused_computation.1.clone.1 | custom fusion | bytes 790528 | tf_op jit(solution)/shard_map/while/body/eval_jaxpr/gather | solution.py:30
  508.6 4.3 fusion.84
  514.9 5.0 gather_fusion.1
  523.5 9.2 %gather_fusion = bf16[1024,32,6]{1,2,0:T(8,128)(2,1)} fusion(bf16[32,6,1088]{0,1,2:T(8,128)(2,1)} %get-tuple-element.825, s32[1024]{0:T(1024)S(1)} %broadcast_clamp_fusion.4), kind=kCustom, calls=%fused_computation.1.clone.1 | custom fusion | bytes 790528 | tf_op jit(solution)/shard_map/while/body/eval_jaxpr/gather | solution.py:30
  532.7 3.6 copy.146
  544.5 4.3 fusion.84
  550.8 5.0 gather_fusion.1
  559.4 9.2 %gather_fusion = bf16[1024,32,6]{1,2,0:T(8,128)(2,1)} fusion(bf16[32,6,1088]{0,1,2:T(8,128)(2,1)} %get-tuple-element.825, s32[1024]{0:T(1024)S(1)} %broadcast_clamp_fusion.4), kind=kCustom, calls=%fused_computation.1.clone.1 | custom fusion | bytes 790528 | tf_op jit(solution)/shard_map/while/body/eval_jaxpr/gather | solution.py:30
  568.6 3.6 copy.146
  580.4 4.3 fusion.84
  585.2 8.8 %scatter_custom_fusion = f32[1920]{0:T(1024)S(1)} fusion(s32[1536]{0:T(1024)} %get-tuple-element.610, f32[1536]{0:T(1024)S(1)} %get-tuple-element.424, f32[]{:T(128)} %constant.148.clone.1), kind=kCustom, calls=%fused_computation.58 | custom fusion | flops 1536 | bytes 8192 | tf_op jit(solution)/shard_map/scatter-add | solution.py:128
  598.3 6.5 %collective-permute-done.8 = f32[640]{0:T(1024)S(1)} collective-permute-done((f32[640]{0:T(1024)S(1)}, f32[640]{0:T(1024)S(1)}, u32[]{:S(2)}, u32[]{:S(2)}) %collective-permute-start.8) | collective-permute-done | bytes 2592 | tf_op jit(solution)/shard_map/ppermute | solution.py:26
  604.8 10.9 %psum.23 = f32[640]{0:T(1024)} all-reduce(f32[640]{0:T(1024)S(1)} %fusion.40), channel_id=1, replica_groups=mesh['dom'=32,'mode'=4] {'mode'}, use_global_device_ids=true, to_apply=%region_11.12 | all-reduce | flops 640 | bytes 5120 | tf_op jit(solution)/shard_map/psum | solution.py:132
  (283 shorter events, 195.5 us)
Async XLA Ops:
  0.6 27.3 %copy-start.2 = (bf16[24,24,1536]{2,1,0:T(8,128)(2,1)S(1)}, bf16[24,24,1536]{2,1,0:T(8,128)(2,1)}, u32[]{:S(2)}) copy-start(bf16[24,24,1536]{2,1,0:T(8,128)(2,1)} %param.16) | copy-start | bytes 5308420
  0.6 13.4 %collective-permute-start = (bf16[32,6,1024]{2,0,1:T(8,128)(2,1)}, bf16[32,6,1024]{2,0,1:T(8,128)(2,1)S(1)}, u32[]{:S(2)}, u32[]{:S(2)}) collective-permute-start(bf16[32,6,1024]{2,0,1:T(8,128)(2,1)} %param.13), channel_id=1, source_target_pairs={{0,1},{1,2},{2,3},{3,0},{4,5},{5,6},{6,7},{7,4},{8,9},{9,10},{10,1... | collective-permute-start | bytes 1179656 | tf_op jit(solution)/shard_map/ppermute | solution.py:52
  14.1 12.1 %copy-start.6 = (bf16[32,6,1024]{2,0,1:T(8,128)(2,1)}, bf16[32,6,1024]{2,0,1:T(8,128)(2,1)S(1)}, u32[]{:S(2)}) copy-start(bf16[32,6,1024]{2,0,1:T(8,128)(2,1)S(1)} %collective-permute-done) | copy-start | bytes 1179652
  14.1 11.6 %collective-permute-start.1 = (bf16[32,6,1024]{2,0,1:T(8,128)(2,1)S(1)}, bf16[32,6,1024]{2,0,1:T(8,128)(2,1)}, u32[]{:S(2)}, u32[]{:S(2)}) collective-permute-start(bf16[32,6,1024]{2,0,1:T(8,128)(2,1)S(1)} %collective-permute-done), channel_id=1, source_target_pairs={{0,1},{1,2},{2,3},{3,0},{4,5},{5,6},{6,7},{7,4},{8,9},{9,10},{10,1... | collective-permute-start | bytes 1179656 | tf_op jit(solution)/shard_map/ppermute | solution.py:52
  14.1 23.4 %collective-permute-start.5 = (f32[640]{0:T(1024)}, f32[640]{0:T(1024)S(1)}, u32[]{:S(2)}, u32[]{:S(2)}) collective-permute-start(f32[640]{0:T(1024)} %param.21), channel_id=1, source_target_pairs={{0,4},{4,8},{8,12},{12,16},{16,20},{20,24},{24,28},{28,32},{32,36}... | collective-permute-start | bytes 7688 | tf_op jit(solution)/shard_map/ppermute | solution.py:15
  16.0 21.5 %collective-permute-start.6 = (f32[640]{0:T(1024)}, f32[640]{0:T(1024)S(1)}, u32[]{:S(2)}, u32[]{:S(2)}) collective-permute-start(f32[640]{0:T(1024)} %param.21), channel_id=1, source_target_pairs={{4,0},{8,4},{12,8},{16,12},{20,16},{24,20},{28,24},{32,28},{36,32}... | collective-permute-start | bytes 7688 | tf_op jit(solution)/shard_map/ppermute | solution.py:18
  25.7 29.0 %collective-permute-start.2 = (bf16[32,6,1024]{2,0,1:T(8,128)(2,1)}, bf16[32,6,1024]{2,0,1:T(8,128)(2,1)}, u32[]{:S(2)}, u32[]{:S(2)}) collective-permute-start(bf16[32,6,1024]{2,0,1:T(8,128)(2,1)} %collective-permute-done.1), channel_id=1, source_target_pairs={{0,1},{1,2},{2,3},{3,0},{4,5},{5,6},{6,7},{7,4},{8,9},{9,10},{10,1... | collective-permute-start | bytes 1179656 | tf_op jit(solution)/shard_map/ppermute | solution.py:52
  28.0 9.0 %copy-start.14 = (f32[128]{0:T(128)S(1)}, f32[128]{0:T(128)}, u32[]{:S(2)}) copy-start(f32[128]{0:T(128)} %param.14) | copy-start | bytes 1540
  28.0 9.6 %copy-start.12 = (f32[640]{0:T(1024)S(1)}, f32[640]{0:T(1024)}, u32[]{:S(2)}) copy-start(f32[640]{0:T(1024)} %param.21) | copy-start | bytes 7684
  37.5 11.7 %copy-start.9 = (f32[1536]{0:T(1024)S(1)}, f32[1536]{0:T(1024)}, u32[]{:S(2)}) copy-start(f32[1536]{0:T(1024)} %param.18) | copy-start | bytes 18436
  70.5 8.0 %collective-permute-start.3 = (bf16[128,6,32]{0,2,1:T(8,128)(2,1)S(1)}, bf16[128,6,32]{0,2,1:T(8,128)(2,1)S(1)}, u32[]{:S(2)}, u32[]{:S(2)}) collective-permute-start(bf16[128,6,32]{0,2,1:T(8,128)(2,1)S(1)} %get-tuple-element.611), channel_id=1, source_target_pairs={{0,4},{4,8},{8,12},{12,16},{16,20},{20,24},{24,28},{28,32},{32,36}... | collective-permute-start | bytes 147464 | tf_op jit(solution)/shard_map/ppermute | solution.py:15
  72.4 6.1 collective-permute-start.4
  78.5 1.1 copy-start.1
  78.5 1.1 copy-start.7
  78.5 1.2 copy-start.8
  87.6 7.3 %copy-start.3 = (bf16[24,24]{1,0:T(8,128)(2,1)S(1)}, bf16[24,24]{1,0:T(8,128)(2,1)}, u32[]{:S(2)}) copy-start(bf16[24,24]{1,0:T(8,128)(2,1)} %param.17) | copy-start | bytes 3460
  115.8 2.1 copy-start.4
  118.5 0.6 copy-start.5
  140.0 2.1 copy-start.4
  142.8 0.6 copy-start.5
  164.3 2.1 copy-start.4
  167.0 0.6 copy-start.5
  188.5 2.1 copy-start.4
  191.3 0.6 copy-start.5
  212.8 2.1 copy-start.4
  215.5 0.6 copy-start.5
  237.0 2.1 copy-start.4
  239.8 0.6 copy-start.5
  367.1 2.6 copy-start.11
  367.1 2.6 copy-start.13
  396.5 2.2 copy-start
  432.4 2.2 copy-start
  468.3 2.2 copy-start
  504.2 2.2 copy-start
  540.1 2.2 copy-start
  576.0 2.2 copy-start
  585.2 30.5 %copy-start.10 = (f32[32]{0:T(128)}, f32[32]{0:T(128)S(1)}, u32[]{:S(2)}) copy-start(f32[32]{0:T(128)S(1)} %get-tuple-element.845) | copy-start | bytes 388
  594.0 4.3 collective-permute-start.7
  595.9 8.9 %collective-permute-start.8 = (f32[640]{0:T(1024)S(1)}, f32[640]{0:T(1024)S(1)}, u32[]{:S(2)}, u32[]{:S(2)}) collective-permute-start(f32[640]{0:T(1024)S(1)} %get-tuple-element.614), channel_id=1, source_target_pairs={{0,4},{4,8},{8,12},{12,16},{16,20},{20,24},{24,28},{28,32},{32,36}... | collective-permute-start | bytes 7688 | tf_op jit(solution)/shard_map/ppermute | solution.py:26
